TPU v7x, 512 devices: a whole 4x4x16 slice. The times are simulated.
512 devices in a mesh: seq: 128 (over z, y, core), grp: 4 (over x).
Axes of the slice: x: 4, y: 4, z: 16, core: 2. Of those that a mesh axis runs over, the one named last changes fastest.
Arguments:
- tokens: bfloat16 [131072, 512], P('seq'), may hold values from -12 to 12
- w_qkv: bfloat16 [3, 512, 512], P(None, None, 'grp'), may hold values from -0.25 to 0.25
- w_out: bfloat16 [512, 512], replicated, may hold values from -0.75 to 0.75
- w_up: bfloat16 [512, 2048], P(None, 'grp'), may hold values from -0.25 to 0.25
- w_down: bfloat16 [2048, 512], P('grp'), may hold values from -0.125 to 0.125
- score_scale: float32 [8], P('grp'), may hold values from 8 to 400
- patch_list: int32 [128, 3], P('seq'), may hold values from 0 to 127, as said below
- relay_dest: int32 [131072, 1], P('seq'), may hold values from 0 to 127; in each aligned block of 1024 rows (0 to 1023, 1024 to 2047, ...) at most 16 rows name the same one
Outputs:
- relayed: bfloat16 [262144, 512], P('seq', 'grp')
Inputs may be any that keep to these rules, and one draw needn't show every extreme that they name: `patch_list`: row p lists patch p first, then 3 - 1 other distinct patches, each at most 2 patches away from p. `relay_dest`: the rows of one block of 1024 tokens name any one block at most 16 times; in every draw some block names some block exactly 16 times.
All inputs are finite; a program needn't handle non-finite values.
Results may differ from a plain program's by a relative error of at most 0.017.
Values may be sent and summed in bfloat16 or wider, within the bound.
A program may use at most 64 MiB of HBM per device.

v0:
```python
import jax
import jax.numpy as jnp
from jax import lax
from jax.sharding import PartitionSpec as P

PATCH = 1024
REACH = 2
NB = 3


def shifted(block, axis, distance):
    devices = range(lax.axis_size(axis))
    route = [(i - distance, i) for i in devices if i - distance in devices]
    return lax.ppermute(block, axis, route)


def layer_norm(token_rows):
    row_mean = jnp.mean(token_rows, axis=-1, keepdims=True)
    spread = jnp.mean(token_rows * token_rows, axis=-1, keepdims=True) - row_mean * row_mean
    return (token_rows - row_mean) * lax.rsqrt(spread + 1e-05)


def unit_heads(values, head_dim):
    shaped = values.reshape(values.shape[0], -1, head_dim)
    scaled = shaped * lax.rsqrt(jnp.mean(shaped * shaped, axis=-1, keepdims=True) + 1e-06)
    return scaled.reshape(values.shape)


def project(token_rows, weights):
    normed = layer_norm(token_rows.astype(jnp.float32)).astype(jnp.bfloat16)
    return jnp.einsum("nd,cde->cne", normed, weights, preferred_element_type=jnp.float32)


def body(tokens, w_qkv, w_out, w_up, w_down, score_scale, patch_list, relay_dest):
    n_seq = lax.axis_size("seq")
    seq_index = lax.axis_index("seq")
    grp_index = lax.axis_index("grp")
    tok_dev, model_width = tokens.shape
    quarter = w_qkv.shape[2]
    heads_dev = score_scale.shape[0]
    head_dim = quarter // heads_dev
    patch_dev = tok_dev // PATCH
    hop_count = -(-REACH // patch_dev)
    offsets = [offset for offset in range(-hop_count, hop_count + 1) if offset != 0]
    own_products = project(tokens, w_qkv)
    queries = unit_heads(own_products[0], head_dim).astype(jnp.bfloat16)
    key_rows = unit_heads(own_products[1], head_dim).astype(jnp.bfloat16)
    value_rows = own_products[2].astype(jnp.bfloat16)
    fetched_pairs = [shifted((key_rows, value_rows), "seq", -offset) for offset in offsets]
    near_keys = [fetched_pair[0] for fetched_pair in fetched_pairs]
    near_values = [fetched_pair[1] for fetched_pair in fetched_pairs]
    window_keys = jnp.concatenate(near_keys[:hop_count] + [key_rows] + near_keys[hop_count:], 0)
    window_values = jnp.concatenate(
        near_values[:hop_count] + [value_rows] + near_values[hop_count:], 0
    )
    window_count = 2 * hop_count + 1
    key_patches = window_keys.reshape(window_count * patch_dev, PATCH, quarter)
    value_patches = window_values.reshape(window_count * patch_dev, PATCH, quarter)
    first_patch = (seq_index - hop_count) * patch_dev
    relative = patch_list - first_patch
    listed_keys = key_patches[relative].reshape(patch_dev, NB * PATCH, quarter)
    listed_values = value_patches[relative].reshape(patch_dev, NB * PATCH, quarter)
    block_rows = min(512, PATCH)
    block_count = PATCH // block_rows
    query_blocks = queries.reshape(patch_dev, block_count, block_rows, quarter)
    factors = score_scale / head_dim

    def attend(item_index):
        patch_index = item_index // (heads_dev * block_count)
        head_index = item_index // block_count % heads_dev
        block_index = item_index % block_count
        query_block = lax.dynamic_slice_in_dim(
            query_blocks[patch_index, block_index], head_index * head_dim, head_dim, 1
        )
        key_block = lax.dynamic_slice_in_dim(
            listed_keys[patch_index], head_index * head_dim, head_dim, 1
        )
        value_block = lax.dynamic_slice_in_dim(
            listed_values[patch_index], head_index * head_dim, head_dim, 1
        )
        scores = lax.dot_general(
            query_block, key_block, (((1,), (1,)), ((), ())), preferred_element_type=jnp.float32
        )
        scores = scores * factors[head_index]
        row_top = jnp.max(scores, axis=1, keepdims=True)
        exponent = jnp.exp(scores - row_top)
        row_total = jnp.sum(exponent, axis=1, keepdims=True)
        weighted = jnp.dot(
            exponent.astype(jnp.bfloat16), value_block, preferred_element_type=jnp.float32
        )
        return (weighted / row_total).astype(jnp.bfloat16)

    attended = lax.map(attend, jnp.arange(patch_dev * heads_dev * block_count, dtype=jnp.int32))
    attended = attended.reshape(patch_dev, heads_dev, block_count, block_rows, head_dim)
    attended = attended.transpose(0, 2, 3, 1, 4).reshape(tok_dev, quarter)
    head_weights = lax.dynamic_slice_in_dim(w_out, grp_index * quarter, quarter, 0)
    partial_proj = jnp.dot(attended, head_weights, preferred_element_type=jnp.float32)
    proj_share = lax.psum_scatter(
        partial_proj.astype(jnp.bfloat16), "grp", scatter_dimension=1, tiled=True
    ).astype(jnp.float32)
    token_share = lax.dynamic_slice_in_dim(tokens, grp_index * quarter, quarter, 1).astype(
        jnp.float32
    )
    resid = (token_share + proj_share).astype(jnp.bfloat16)
    resid_wide = resid.astype(jnp.float32)
    row_sums = lax.psum(
        (jnp.sum(resid_wide, axis=1), jnp.sum(resid_wide * resid_wide, axis=1)), "grp"
    )
    row_mean = row_sums[0] / model_width
    spread = row_sums[1] / model_width - row_mean * row_mean
    normed_share = ((resid_wide - row_mean[:, None]) * lax.rsqrt(spread + 1e-05)[:, None]).astype(
        jnp.bfloat16
    )
    hidden_pre = jnp.dot(
        lax.all_gather(normed_share, "grp", axis=1, tiled=True),
        w_up,
        preferred_element_type=jnp.float32,
    )
    hidden = jax.nn.gelu(hidden_pre).astype(jnp.bfloat16)
    partial_down = jnp.dot(hidden, w_down, preferred_element_type=jnp.float32)
    down_share = lax.psum_scatter(
        partial_down.astype(jnp.bfloat16), "grp", scatter_dimension=1, tiled=True
    ).astype(jnp.float32)
    out_rows = (resid.astype(jnp.float32) + down_share).astype(jnp.bfloat16)
    capacity = 2 * tok_dev // n_seq
    destination = relay_dest[:, 0]
    onehot = (destination[:, None] == jnp.arange(n_seq, dtype=jnp.int32)[None, :]).astype(jnp.int32)
    before = jnp.cumsum(onehot, axis=0) - onehot
    rank_rows = jnp.sum(before * onehot, axis=1)
    slot_index = destination * capacity + rank_rows
    send_buffer = jnp.zeros((n_seq * capacity, quarter), jnp.bfloat16).at[slot_index].set(out_rows)
    received = lax.all_to_all(
        send_buffer.reshape(n_seq, capacity, quarter),
        "seq",
        split_axis=0,
        concat_axis=0,
        tiled=True,
    )
    return received.reshape(n_seq * capacity, quarter)


def solution(mesh):
    return jax.shard_map(
        body,
        mesh=mesh,
        in_specs=(
            P("seq", None),
            P(None, None, "grp"),
            P(),
            P(None, "grp"),
            P("grp", None),
            P("grp"),
            P("seq", None),
            P("seq", None),
        ),
        out_specs=P("seq", "grp"),
        check_vma=False,
    )
```

profile of v0, /device:TPU:33, one launch (start us, length us, event | category | flops | bytes accessed | tf_op | source)
XLA Modules:
  0.0 282.7 jit_solution(186942135605513350)
XLA Ops:
  6.5 1.6 convert_reduce_fusion
  8.2 1.2 copy.24
  9.4 2.0 fusion.36
  11.4 1.2 slice_multiply_fusion
  12.5 1.1 reduce_sum.83
  13.7 3.2 %collective-permute-start = (bf16[1024,128]{0,1:T(8,128)(2,1)S(1)}, bf16[1024,128]{0,1:T(8,128)(2,1)}, u32[]{:S(2)}, u32[]{:S(2)}) collective-permute-start(bf16[1024,128]{0,1:T(8,128)(2,1)S(1)} %fusion.50), channel_id=1, source_target_pairs={{0,8},{4,12},{8,16},{12,20},{16,24},{20,28},{24,32},{28,36},{32,40... | collective-permute-start | bytes 786440 | tf_op jit(solution)/shard_map/ppermute | solution.py:14
  16.9 4.0 %collective-permute-start.1 = (bf16[1024,128]{0,1:T(8,128)(2,1)S(1)}, bf16[1024,128]{0,1:T(8,128)(2,1)}, u32[]{:S(2)}, u32[]{:S(2)}) collective-permute-start(bf16[1024,128]{0,1:T(8,128)(2,1)S(1)} %fusion.50), channel_id=1, source_target_pairs={{0,4},{4,8},{8,12},{12,16},{16,20},{20,24},{24,28},{28,32},{32,36}... | collective-permute-start | bytes 786440 | tf_op jit(solution)/shard_map/ppermute | solution.py:14
  21.0 1.9 collective-permute-start.2
  22.9 4.2 %collective-permute-start.3 = (bf16[1024,128]{0,1:T(8,128)(2,1)S(1)}, bf16[1024,128]{0,1:T(8,128)(2,1)}, u32[]{:S(2)}, u32[]{:S(2)}) collective-permute-start(bf16[1024,128]{0,1:T(8,128)(2,1)S(1)} %fusion.50), channel_id=1, source_target_pairs={{8,0},{12,4},{16,8},{20,12},{24,16},{28,20},{32,24},{36,28},{40,32... | collective-permute-start | bytes 786440 | tf_op jit(solution)/shard_map/ppermute | solution.py:14
  27.9 1.9 collective-permute-start.4
  31.2 3.9 %collective-permute-start.5 = (bf16[1024,128]{0,1:T(8,128)(2,1)}, bf16[1024,128]{0,1:T(8,128)(2,1)S(1)}, u32[]{:S(2)}, u32[]{:S(2)}) collective-permute-start(bf16[1024,128]{0,1:T(8,128)(2,1)} %fusion.53), channel_id=1, source_target_pairs={{0,4},{4,8},{8,12},{12,16},{16,20},{20,24},{24,28},{28,32},{32,36}... | collective-permute-start | bytes 786440 | tf_op jit(solution)/shard_map/ppermute | solution.py:14
  35.1 1.0 constant_dynamic-update-slice_fusion.4
  36.1 2.3 collective-permute-start.6
  38.4 1.0 constant_dynamic-update-slice_fusion.3
  39.4 5.4 %collective-permute-start.7 = (bf16[1024,128]{0,1:T(8,128)(2,1)}, bf16[1024,128]{0,1:T(8,128)(2,1)S(1)}, u32[]{:S(2)}, u32[]{:S(2)}) collective-permute-start(bf16[1024,128]{0,1:T(8,128)(2,1)} %fusion.53), channel_id=1, source_target_pairs={{8,0},{12,4},{16,8},{20,12},{24,16},{28,20},{32,24},{36,28},{40,32... | collective-permute-start | bytes 786440 | tf_op jit(solution)/shard_map/ppermute | solution.py:14
  44.8 1.7 constant_dynamic-update-slice_fusion.9
  47.4 1.0 constant_dynamic-update-slice_fusion
  48.4 1.0 copy-done.2
  50.2 1.8 copy.25
  52.0 1.8 constant_dynamic-update-slice_fusion.7
  55.4 2.4 copy.26
  58.5 2.0 gather_fusion.1
  60.5 39.8 %while.13 = (s32[]{:T(128)}, bf16[4,512,64]{1,2,0:T(8,128)(2,1)S(1)}, s32[4]{0:T(128)S(1)}, bf16[1,2,512,128]{2,1,3,0:T(2,128)(2,1)S(1)}, bf16[1,3072,128]{2,1,0...) while((s32[]{:T(128)}, ...), condition=%wide.region_10.11_spmd, body=%wide.region_7.10_spmd.sunk | while | flops 415300672 | bytes 20851312 | solution.py:93
  64.7 1.8 multiply_reduce_fusion.2
  66.5 1.8 fusion.78
  68.3 2.2 fusion.79
  74.6 1.8 multiply_reduce_fusion.2
  76.4 1.8 fusion.78
  78.2 2.2 fusion.79
  84.6 1.8 multiply_reduce_fusion.2
  86.4 1.8 fusion.78
  88.2 2.2 fusion.79
  94.6 1.8 multiply_reduce_fusion.2
  96.4 1.8 fusion.78
  98.2 2.2 fusion.79
  101.2 1.3 copy.29
  102.6 34.9 %reduce-scatter.7.cloned.1.call-done = bf16[128,1024]{1,0:T(8,128)(2,1)} async-done(((bf16[512,1024]{1,0:T(8,128)(2,1)}), bf16[128,1024]{1,0:T(8,128)(2,1)}) %reduce-scatter.7.cloned.1.call-update) | async-done | bytes 262160
  137.5 1.1 copy.30
  138.7 1.3 convert_reduce_fusion.1
  140.0 6.6 %all-reduce = (f32[1024]{0:T(1024)S(1)}, f32[1024]{0:T(1024)S(1)}) all-reduce(f32[1024]{0:T(1024)S(1)} %get-tuple-element.144, f32[1024]{0:T(1024)S(1)} %get-tuple-element.143), channel_id=1, replica_groups=mesh['seq'=128,'grp'=4] {'grp'}, use_global_device_ids=true, to_apply=%region_15.16 | all-reduce | flops 2048 | bytes 16384 | tf_op jit(solution)/shard_map/psum | solution.py:106
  146.6 1.0 fusion.45
  147.9 35.5 %all-gather.2.cloned.1.call-done = bf16[1024,512]{1,0:T(8,128)(2,1)} async-done(((bf16[1024,128]{1,0:T(8,128)(2,1)}), bf16[1024,512]{1,0:T(8,128)(2,1)}) %all-gather.2.cloned.1.call-update) | async-done | bytes 1048592 | tf_op jit(solution)/shard_map/all_gather | solution.py:115
  183.4 2.7 convolution_convert_fusion.1
  186.1 1.3 copy.31
  188.4 31.1 %reduce-scatter.9.cloned.1.call-done = bf16[128,1024]{1,0:T(8,128)(2,1)} async-done(((bf16[512,1024]{1,0:T(8,128)(2,1)}), bf16[128,1024]{1,0:T(8,128)(2,1)}) %reduce-scatter.9.cloned.1.call-update) | async-done | bytes 262160
  219.5 1.1 copy.32
  220.6 3.4 %scatter_custom_fusion = bf16[2048,128]{1,0:T(8,128)(2,1)S(1)} fusion(s32[1024]{0:T(1024)S(1)} %bitcast.114, bf16[1024,128]{1,0:T(8,128)(2,1)S(1)} %get-tuple-element.161, bf16[1024,128]{1,0:T(8,128)(2,1)S(1)} %copy.32, bf16[]{:T(256)} %constant.173.clone.1), kind=kCustom, calls=%fused_computation.67 | custom fusion | flops 524288 | bytes 1048578 | tf_op jit(solution)/shard_map/scatter | solution.py:131
  224.0 51.4 %all_to_all.5 = bf16[128,16,128]{2,1,0:T(8,128)(2,1)S(1)} all-to-all(bf16[128,16,128]{2,1,0:T(8,128)(2,1)S(1)} %bitcast.103), channel_id=1, replica_groups=mesh['seq'=128,'grp'=4] {'seq'}, dimensions={0} | all-to-all | bytes 1048576 | tf_op jit(solution)/shard_map/all_to_all | solution.py:132
  (80 shorter events, 14.7 us)
Async XLA Ops:
  6.5 94.2 %copy-start = (bf16[512,512]{1,0:T(8,128)(2,1)S(1)}, bf16[512,512]{1,0:T(8,128)(2,1)}, u32[]{:S(2)}) copy-start(bf16[512,512]{1,0:T(8,128)(2,1)} %param.12) | copy-start | bytes 1572868
  6.5 131.0 %reduce-scatter.7.cloned.1.call-start = ((), (), s32[]{:S(2)}) async-start(), calls=%async_computation.4 | async-start | bytes 1310720
  11.4 16.5 %copy-start.1 = (f32[1024,384]{0,1}, f32[1024,384]{0,1:S(1)}, u32[]{:S(2)}) copy-start(f32[1024,384]{0,1:S(1)} %fusion.36) | copy-start | bytes 4718596
  13.7 17.2 %copy-start.6 = (f32[2]{0:T(128)S(1)}, f32[2]{0:T(128)}, u32[]{:S(2)}) copy-start(f32[2]{0:T(128)} %param.15) | copy-start | bytes 28
  13.7 17.5 %collective-permute-start = (bf16[1024,128]{0,1:T(8,128)(2,1)S(1)}, bf16[1024,128]{0,1:T(8,128)(2,1)}, u32[]{:S(2)}, u32[]{:S(2)}) collective-permute-start(bf16[1024,128]{0,1:T(8,128)(2,1)S(1)} %fusion.50), channel_id=1, source_target_pairs={{0,8},{4,12},{8,16},{12,20},{16,24},{20,28},{24,32},{28,36},{32,40... | collective-permute-start | bytes 786440 | tf_op jit(solution)/shard_map/ppermute | solution.py:14
  16.9 19.2 %collective-permute-start.1 = (bf16[1024,128]{0,1:T(8,128)(2,1)S(1)}, bf16[1024,128]{0,1:T(8,128)(2,1)}, u32[]{:S(2)}, u32[]{:S(2)}) collective-permute-start(bf16[1024,128]{0,1:T(8,128)(2,1)S(1)} %fusion.50), channel_id=1, source_target_pairs={{0,4},{4,8},{8,12},{12,16},{16,20},{20,24},{24,28},{28,32},{32,36}... | collective-permute-start | bytes 786440 | tf_op jit(solution)/shard_map/ppermute | solution.py:14
  21.0 25.5 %collective-permute-start.2 = (bf16[1024,128]{0,1:T(8,128)(2,1)S(1)}, bf16[1024,128]{0,1:T(8,128)(2,1)}, u32[]{:S(2)}, u32[]{:S(2)}) collective-permute-start(bf16[1024,128]{0,1:T(8,128)(2,1)S(1)} %fusion.50), channel_id=1, source_target_pairs={{4,0},{8,4},{12,8},{16,12},{20,16},{24,20},{28,24},{32,28},{36,32}... | collective-permute-start | bytes 786440 | tf_op jit(solution)/shard_map/ppermute | solution.py:14
  22.9 24.5 %collective-permute-start.3 = (bf16[1024,128]{0,1:T(8,128)(2,1)S(1)}, bf16[1024,128]{0,1:T(8,128)(2,1)}, u32[]{:S(2)}, u32[]{:S(2)}) collective-permute-start(bf16[1024,128]{0,1:T(8,128)(2,1)S(1)} %fusion.50), channel_id=1, source_target_pairs={{8,0},{12,4},{16,8},{20,12},{24,16},{28,20},{32,24},{36,28},{40,32... | collective-permute-start | bytes 786440 | tf_op jit(solution)/shard_map/ppermute | solution.py:14
  27.9 11.5 %collective-permute-start.4 = (bf16[1024,128]{0,1:T(8,128)(2,1)}, bf16[1024,128]{0,1:T(8,128)(2,1)}, u32[]{:S(2)}, u32[]{:S(2)}) collective-permute-start(bf16[1024,128]{0,1:T(8,128)(2,1)} %fusion.53), channel_id=1, source_target_pairs={{0,8},{4,12},{8,16},{12,20},{16,24},{20,28},{24,32},{28,36},{32,40... | collective-permute-start | bytes 786440 | tf_op jit(solution)/shard_map/ppermute | solution.py:14
  29.8 1.3 copy-start.7
  31.2 17.3 %collective-permute-start.5 = (bf16[1024,128]{0,1:T(8,128)(2,1)}, bf16[1024,128]{0,1:T(8,128)(2,1)S(1)}, u32[]{:S(2)}, u32[]{:S(2)}) collective-permute-start(bf16[1024,128]{0,1:T(8,128)(2,1)} %fusion.53), channel_id=1, source_target_pairs={{0,4},{4,8},{8,12},{12,16},{16,20},{20,24},{24,28},{28,32},{32,36}... | collective-permute-start | bytes 786440 | tf_op jit(solution)/shard_map/ppermute | solution.py:14
  36.1 17.7 %collective-permute-start.6 = (bf16[1024,128]{0,1:T(8,128)(2,1)}, bf16[1024,128]{0,1:T(8,128)(2,1)S(1)}, u32[]{:S(2)}, u32[]{:S(2)}) collective-permute-start(bf16[1024,128]{0,1:T(8,128)(2,1)} %fusion.53), channel_id=1, source_target_pairs={{4,0},{8,4},{12,8},{16,12},{20,16},{24,20},{28,24},{32,28},{36,32}... | collective-permute-start | bytes 786440 | tf_op jit(solution)/shard_map/ppermute | solution.py:14
  39.4 15.2 %collective-permute-start.7 = (bf16[1024,128]{0,1:T(8,128)(2,1)}, bf16[1024,128]{0,1:T(8,128)(2,1)S(1)}, u32[]{:S(2)}, u32[]{:S(2)}) collective-permute-start(bf16[1024,128]{0,1:T(8,128)(2,1)} %fusion.53), channel_id=1, source_target_pairs={{8,0},{12,4},{16,8},{20,12},{24,16},{28,20},{32,24},{36,28},{40,32... | collective-permute-start | bytes 786440 | tf_op jit(solution)/shard_map/ppermute | solution.py:14
  48.4 1.1 copy-start.2
  102.5 80.9 %copy-start.4 = (bf16[512,512]{1,0:T(8,128)(2,1)S(1)}, bf16[512,512]{1,0:T(8,128)(2,1)}, u32[]{:S(2)}) copy-start(bf16[512,512]{1,0:T(8,128)(2,1)} %param.14) | copy-start | bytes 1572868
  102.5 80.9 %copy-start.5 = (bf16[512,512]{1,0:T(8,128)(2,1)S(1)}, bf16[512,512]{1,0:T(8,128)(2,1)}, u32[]{:S(2)}) copy-start(bf16[512,512]{1,0:T(8,128)(2,1)} %param.13) | copy-start | bytes 1572868
  102.5 80.9 %all-gather.2.cloned.1.call-start = ((), (), s32[]{:S(2)}) async-start(), calls=%async_computation.3 | async-start | bytes 1310720 | tf_op jit(solution)/shard_map/all_gather | solution.py:115
  147.7 71.8 %reduce-scatter.9.cloned.1.call-start = ((), (), s32[]{:S(2)}) async-start(), calls=%async_computation.5 | async-start | bytes 1310720
  186.1 1.4 copy-start.3
Sparse Core Ops, SparseCore 0:
  102.7 34.8 reduce-scatter.6
  147.8 35.6 all-gather.1
  187.6 31.8 reduce-scatter.8
where the time goes:
time: 284 us; the launch traced here: 283 us
  waiting for transfers between devices  102 us (36%)
  blocking collectives  58 us (20%)
  local copies, waits for them, and re-layouts  32.6 us (11%)
  starting transfers between devices  27.1 us (10%)
  matrix products  21.2 us (7%)
  other arithmetic  17.8 us (6%)
  between operations  13.6 us (5%)
  loops' own time  10.7 us (4%)
    unnamed x5, waiting for transfers between devices  66.1 us
    all_to_all x1, blocking collectives, body(): lax.all_to_all(send_buffer.reshape(n_seq, capacity, quarter), 'seq', spli...  51.4 us
    all_gather x1, waiting for transfers between devices, body(): lax.all_gather(normed_share, 'grp', axis=1, tiled=True)  35.5 us
    ppermute x8, starting transfers between devices, shifted(): return lax.ppermute(block, axis, route)  26.9 us
    unnamed x31, local copies, waits for them, and re-layouts  15.9 us
    another operation x1, loops' own time, body(): lax.map(attend, jnp.arange(patch_dev * heads_dev * block_count, dtype=jnp...  10.7 us
    dot_general x4, matrix products, attend(): jnp.dot(exponent.astype(jnp.bfloat16), value_block, preferred_element_typ...  8.91 us
    dot_general x4, matrix products, attend(): lax.dot_general(query_block, key_block, (((1,), (1,)), ((), ())), preferr...  7.2 us
  transfers between devices with their start and end apart: 11, of which 3 were waited for; matrix products, arithmetic and copies ran while one was open for 5% of the time, Pallas kernels for 0%

commit v1 on v0

--- a/solution.py
+++ b/solution.py
@@ -6,6 +6,13 @@
 PATCH = 1024
 REACH = 2
 NB = 3
+
+
+def all_by_exchange(x, axis, dim):
+    peers = lax.axis_size(axis)
+    blocks = jnp.stack([x for _ in range(peers)])
+    blocks = lax.all_to_all(blocks, axis, split_axis=0, concat_axis=0)
+    return jnp.concatenate(blocks, axis=dim)
 
 
 def shifted(block, axis, distance):
@@ -112,9 +119,7 @@
         jnp.bfloat16
     )
     hidden_pre = jnp.dot(
-        lax.all_gather(normed_share, "grp", axis=1, tiled=True),
-        w_up,
-        preferred_element_type=jnp.float32,
+        all_by_exchange(normed_share, "grp", 1), w_up, preferred_element_type=jnp.float32
     )
     hidden = jax.nn.gelu(hidden_pre).astype(jnp.bfloat16)
     partial_down = jnp.dot(hidden, w_down, preferred_element_type=jnp.float32)

time: 284 us -> 263 us (0.926)
  waiting for transfers between devices: 102 us -> 68.2 us
  blocking collectives: 58 us -> 71.3 us
    all_gather x1 -> x0, waiting for transfers between devices: 35.5 us -> none  [body(): lax.all_gather(normed_share, 'grp', axis=1, tiled=True)]
    all_to_all x0 -> x1, blocking collectives: none -> 13.2 us  [all_by_exchange(): blocks = lax.all_to_all(blocks, axis, split_axis=0, concat_axis=0)]
    unnamed x5 -> x4, waiting for transfers between devices: 66.1 us -> 68.2 us
    unnamed x31 -> x29, local copies, waits for them, and re-layouts: 15.9 us -> 15.9 us
  transfers between devices with their start and end apart: 11 -> 10, of which waited for: 3 -> 2; matrix products, arithmetic and copies ran while one was open for 5% -> 5% of each run, Pallas kernels for 0% -> 0%
where the time goes in v1:
time: 263 us; the launch traced here: 262 us
  blocking collectives  71.3 us (27%)
  waiting for transfers between devices  68.2 us (26%)
  local copies, waits for them, and re-layouts  32.8 us (12%)
  starting transfers between devices  26.9 us (10%)
  matrix products  21.1 us (8%)
  other arithmetic  17.1 us (7%)
  between operations  13.9 us (5%)
  loops' own time  10.7 us (4%)
    unnamed x4, waiting for transfers between devices  68.2 us
    all_to_all x1, blocking collectives, body(): lax.all_to_all(send_buffer.reshape(n_seq, capacity, quarter), 'seq', spli...  51.5 us
    ppermute x8, starting transfers between devices, shifted(): return lax.ppermute(block, axis, route)  26.9 us
    unnamed x29, local copies, waits for them, and re-layouts  15.9 us
    all_to_all x1, blocking collectives, all_by_exchange(): blocks = lax.all_to_all(blocks, axis, split_axis=0, concat_axis=0)  13.2 us
    another operation x1, loops' own time, body(): lax.map(attend, jnp.arange(patch_dev * heads_dev * block_count, dtype=jnp...  10.7 us
    dot_general x4, matrix products, attend(): jnp.dot(exponent.astype(jnp.bfloat16), value_block, preferred_element_typ...  8.91 us
    dot_general x4, matrix products, attend(): lax.dot_general(query_block, key_block, (((1,), (1,)), ((), ())), preferr...  7.2 us
  transfers between devices with their start and end apart: 10, of which 2 were waited for; matrix products, arithmetic and copies ran while one was open for 5% of the time, Pallas kernels for 0%

profile of v1, /device:TPU:33, one launch (start us, length us, event | category | flops | bytes accessed | tf_op | source)
XLA Modules:
  0.0 262.1 jit_solution(10282448863749288252)
XLA Ops:
  6.5 1.6 convert_reduce_fusion
  8.2 1.2 copy.25
  9.4 2.0 fusion.36
  11.4 1.2 slice_multiply_fusion
  12.5 1.1 reduce_sum.83
  13.7 3.2 %collective-permute-start = (bf16[1024,128]{0,1:T(8,128)(2,1)S(1)}, bf16[1024,128]{0,1:T(8,128)(2,1)}, u32[]{:S(2)}, u32[]{:S(2)}) collective-permute-start(bf16[1024,128]{0,1:T(8,128)(2,1)S(1)} %fusion.50), channel_id=1, source_target_pairs={{0,8},{4,12},{8,16},{12,20},{16,24},{20,28},{24,32},{28,36},{32,40... | collective-permute-start | bytes 786440 | tf_op jit(solution)/shard_map/ppermute | solution.py:21
  16.9 4.0 %collective-permute-start.1 = (bf16[1024,128]{0,1:T(8,128)(2,1)S(1)}, bf16[1024,128]{0,1:T(8,128)(2,1)}, u32[]{:S(2)}, u32[]{:S(2)}) collective-permute-start(bf16[1024,128]{0,1:T(8,128)(2,1)S(1)} %fusion.50), channel_id=1, source_target_pairs={{0,4},{4,8},{8,12},{12,16},{16,20},{20,24},{24,28},{28,32},{32,36}... | collective-permute-start | bytes 786440 | tf_op jit(solution)/shard_map/ppermute | solution.py:21
  21.0 1.9 collective-permute-start.2
  22.9 4.2 %collective-permute-start.3 = (bf16[1024,128]{0,1:T(8,128)(2,1)S(1)}, bf16[1024,128]{0,1:T(8,128)(2,1)}, u32[]{:S(2)}, u32[]{:S(2)}) collective-permute-start(bf16[1024,128]{0,1:T(8,128)(2,1)S(1)} %fusion.50), channel_id=1, source_target_pairs={{8,0},{12,4},{16,8},{20,12},{24,16},{28,20},{32,24},{36,28},{40,32... | collective-permute-start | bytes 786440 | tf_op jit(solution)/shard_map/ppermute | solution.py:21
  27.9 1.9 collective-permute-start.4
  31.2 3.9 %collective-permute-start.5 = (bf16[1024,128]{0,1:T(8,128)(2,1)}, bf16[1024,128]{0,1:T(8,128)(2,1)S(1)}, u32[]{:S(2)}, u32[]{:S(2)}) collective-permute-start(bf16[1024,128]{0,1:T(8,128)(2,1)} %fusion.53), channel_id=1, source_target_pairs={{0,4},{4,8},{8,12},{12,16},{16,20},{20,24},{24,28},{28,32},{32,36}... | collective-permute-start | bytes 786440 | tf_op jit(solution)/shard_map/ppermute | solution.py:21
  35.1 1.0 constant_dynamic-update-slice_fusion.4
  36.1 2.3 collective-permute-start.6
  38.4 1.0 constant_dynamic-update-slice_fusion.3
  39.4 5.4 %collective-permute-start.7 = (bf16[1024,128]{0,1:T(8,128)(2,1)}, bf16[1024,128]{0,1:T(8,128)(2,1)S(1)}, u32[]{:S(2)}, u32[]{:S(2)}) collective-permute-start(bf16[1024,128]{0,1:T(8,128)(2,1)} %fusion.53), channel_id=1, source_target_pairs={{8,0},{12,4},{16,8},{20,12},{24,16},{28,20},{32,24},{36,28},{40,32... | collective-permute-start | bytes 786440 | tf_op jit(solution)/shard_map/ppermute | solution.py:21
  44.8 1.7 constant_dynamic-update-slice_fusion.9
  46.5 1.0 constant_dynamic-update-slice_fusion.1
  47.4 1.0 constant_dynamic-update-slice_fusion
  48.4 1.0 copy-done.2
  50.2 1.8 copy.26
  52.0 1.8 constant_dynamic-update-slice_fusion.7
  55.4 2.4 copy.27
  58.5 2.0 gather_fusion.1
  60.5 39.8 %while.13 = (s32[]{:T(128)}, bf16[4,512,64]{1,2,0:T(8,128)(2,1)S(1)}, s32[4]{0:T(128)S(1)}, bf16[1,2,512,128]{2,1,3,0:T(2,128)(2,1)S(1)}, bf16[1,3072,128]{2,1,0...) while((s32[]{:T(128)}, ...), condition=%wide.region_10.11_spmd, body=%wide.region_7.10_spmd.sunk | while | flops 415300672 | bytes 20851312 | solution.py:100
  64.7 1.8 multiply_reduce_fusion.2
  66.5 1.8 fusion.78
  68.3 2.2 fusion.79
  74.6 1.8 multiply_reduce_fusion.2
  76.4 1.8 fusion.78
  78.2 2.2 fusion.79
  84.6 1.8 multiply_reduce_fusion.2
  86.4 1.8 fusion.78
  88.2 2.2 fusion.79
  94.6 1.8 multiply_reduce_fusion.2
  96.4 1.8 fusion.78
  98.2 2.2 fusion.79
  101.2 1.3 copy.31
  102.6 34.9 %reduce-scatter.7.cloned.1.call-done = bf16[128,1024]{1,0:T(8,128)(2,1)} async-done(((bf16[512,1024]{1,0:T(8,128)(2,1)}), bf16[128,1024]{1,0:T(8,128)(2,1)}) %reduce-scatter.7.cloned.1.call-update) | async-done | bytes 262160
  137.5 1.1 copy.32
  138.7 1.3 convert_reduce_fusion.1
  140.0 6.6 %all-reduce = (f32[1024]{0:T(1024)S(1)}, f32[1024]{0:T(1024)S(1)}) all-reduce(f32[1024]{0:T(1024)S(1)} %get-tuple-element.144, f32[1024]{0:T(1024)S(1)} %get-tuple-element.143), channel_id=1, replica_groups=mesh['seq'=128,'grp'=4] {'grp'}, use_global_device_ids=true, to_apply=%region_15.16 | all-reduce | flops 2048 | bytes 16384 | tf_op jit(solution)/shard_map/psum | solution.py:113
  147.2 13.2 %all_to_all.10 = bf16[4,1024,128]{1,2,0:T(8,128)(2,1)S(1)} all-to-all(bf16[4,1024,128]{1,2,0:T(8,128)(2,1)S(1)} %stack.2), channel_id=1, replica_groups=mesh['seq'=128,'grp'=4] {'grp'}, dimensions={0} | all-to-all | bytes 2097152 | tf_op jit(solution)/shard_map/all_to_all | solution.py:14
  160.4 2.5 convolution_convert_fusion.1
  163.0 1.3 copy.33
  165.3 33.2 %reduce-scatter.9.cloned.1.call-done = bf16[128,1024]{1,0:T(8,128)(2,1)} async-done(((bf16[512,1024]{1,0:T(8,128)(2,1)}), bf16[128,1024]{1,0:T(8,128)(2,1)}) %reduce-scatter.9.cloned.1.call-update) | async-done | bytes 262160
  198.5 1.1 copy.34
  199.6 3.4 %scatter_custom_fusion = bf16[2048,128]{1,0:T(8,128)(2,1)S(1)} fusion(s32[1024]{0:T(1024)S(1)} %bitcast.118, bf16[1024,128]{1,0:T(8,128)(2,1)S(1)} %get-tuple-element.161, bf16[1024,128]{1,0:T(8,128)(2,1)S(1)} %copy.34, bf16[]{:T(256)} %constant.173.clone.1), kind=kCustom, calls=%fused_computation.67 | custom fusion | flops 524288 | bytes 1048578 | tf_op jit(solution)/shard_map/scatter | solution.py:136
  203.0 51.5 %all_to_all.11 = bf16[128,16,128]{2,1,0:T(8,128)(2,1)S(1)} all-to-all(bf16[128,16,128]{2,1,0:T(8,128)(2,1)S(1)} %bitcast.106), channel_id=1, replica_groups=mesh['seq'=128,'grp'=4] {'seq'}, dimensions={0} | all-to-all | bytes 1048576 | tf_op jit(solution)/shard_map/all_to_all | solution.py:137
  (78 shorter events, 14.1 us)
Async XLA Ops:
  6.5 94.2 %copy-start = (bf16[512,512]{1,0:T(8,128)(2,1)S(1)}, bf16[512,512]{1,0:T(8,128)(2,1)}, u32[]{:S(2)}) copy-start(bf16[512,512]{1,0:T(8,128)(2,1)} %param.12) | copy-start | bytes 1572868
  6.5 131.0 %reduce-scatter.7.cloned.1.call-start = ((), (), s32[]{:S(2)}) async-start(), calls=%async_computation.4 | async-start | bytes 1310720
  11.4 16.5 %copy-start.1 = (f32[1024,384]{0,1}, f32[1024,384]{0,1:S(1)}, u32[]{:S(2)}) copy-start(f32[1024,384]{0,1:S(1)} %fusion.36) | copy-start | bytes 4718596
  13.7 17.2 %copy-start.5 = (f32[2]{0:T(128)S(1)}, f32[2]{0:T(128)}, u32[]{:S(2)}) copy-start(f32[2]{0:T(128)} %param.15) | copy-start | bytes 28
  13.7 17.5 %collective-permute-start = (bf16[1024,128]{0,1:T(8,128)(2,1)S(1)}, bf16[1024,128]{0,1:T(8,128)(2,1)}, u32[]{:S(2)}, u32[]{:S(2)}) collective-permute-start(bf16[1024,128]{0,1:T(8,128)(2,1)S(1)} %fusion.50), channel_id=1, source_target_pairs={{0,8},{4,12},{8,16},{12,20},{16,24},{20,28},{24,32},{28,36},{32,40... | collective-permute-start | bytes 786440 | tf_op jit(solution)/shard_map/ppermute | solution.py:21
  16.9 19.2 %collective-permute-start.1 = (bf16[1024,128]{0,1:T(8,128)(2,1)S(1)}, bf16[1024,128]{0,1:T(8,128)(2,1)}, u32[]{:S(2)}, u32[]{:S(2)}) collective-permute-start(bf16[1024,128]{0,1:T(8,128)(2,1)S(1)} %fusion.50), channel_id=1, source_target_pairs={{0,4},{4,8},{8,12},{12,16},{16,20},{20,24},{24,28},{28,32},{32,36}... | collective-permute-start | bytes 786440 | tf_op jit(solution)/shard_map/ppermute | solution.py:21
  21.0 25.5 %collective-permute-start.2 = (bf16[1024,128]{0,1:T(8,128)(2,1)S(1)}, bf16[1024,128]{0,1:T(8,128)(2,1)}, u32[]{:S(2)}, u32[]{:S(2)}) collective-permute-start(bf16[1024,128]{0,1:T(8,128)(2,1)S(1)} %fusion.50), channel_id=1, source_target_pairs={{4,0},{8,4},{12,8},{16,12},{20,16},{24,20},{28,24},{32,28},{36,32}... | collective-permute-start | bytes 786440 | tf_op jit(solution)/shard_map/ppermute | solution.py:21
  22.9 24.5 %collective-permute-start.3 = (bf16[1024,128]{0,1:T(8,128)(2,1)S(1)}, bf16[1024,128]{0,1:T(8,128)(2,1)}, u32[]{:S(2)}, u32[]{:S(2)}) collective-permute-start(bf16[1024,128]{0,1:T(8,128)(2,1)S(1)} %fusion.50), channel_id=1, source_target_pairs={{8,0},{12,4},{16,8},{20,12},{24,16},{28,20},{32,24},{36,28},{40,32... | collective-permute-start | bytes 786440 | tf_op jit(solution)/shard_map/ppermute | solution.py:21
  27.9 11.5 %collective-permute-start.4 = (bf16[1024,128]{0,1:T(8,128)(2,1)}, bf16[1024,128]{0,1:T(8,128)(2,1)}, u32[]{:S(2)}, u32[]{:S(2)}) collective-permute-start(bf16[1024,128]{0,1:T(8,128)(2,1)} %fusion.53), channel_id=1, source_target_pairs={{0,8},{4,12},{8,16},{12,20},{16,24},{20,28},{24,32},{28,36},{32,40... | collective-permute-start | bytes 786440 | tf_op jit(solution)/shard_map/ppermute | solution.py:21
  29.8 1.3 copy-start.6
  31.2 17.3 %collective-permute-start.5 = (bf16[1024,128]{0,1:T(8,128)(2,1)}, bf16[1024,128]{0,1:T(8,128)(2,1)S(1)}, u32[]{:S(2)}, u32[]{:S(2)}) collective-permute-start(bf16[1024,128]{0,1:T(8,128)(2,1)} %fusion.53), channel_id=1, source_target_pairs={{0,4},{4,8},{8,12},{12,16},{16,20},{20,24},{24,28},{28,32},{32,36}... | collective-permute-start | bytes 786440 | tf_op jit(solution)/shard_map/ppermute | solution.py:21
  36.1 17.7 %collective-permute-start.6 = (bf16[1024,128]{0,1:T(8,128)(2,1)}, bf16[1024,128]{0,1:T(8,128)(2,1)S(1)}, u32[]{:S(2)}, u32[]{:S(2)}) collective-permute-start(bf16[1024,128]{0,1:T(8,128)(2,1)} %fusion.53), channel_id=1, source_target_pairs={{4,0},{8,4},{12,8},{16,12},{20,16},{24,20},{28,24},{32,28},{36,32}... | collective-permute-start | bytes 786440 | tf_op jit(solution)/shard_map/ppermute | solution.py:21
  39.4 15.2 %collective-permute-start.7 = (bf16[1024,128]{0,1:T(8,128)(2,1)}, bf16[1024,128]{0,1:T(8,128)(2,1)S(1)}, u32[]{:S(2)}, u32[]{:S(2)}) collective-permute-start(bf16[1024,128]{0,1:T(8,128)(2,1)} %fusion.53), channel_id=1, source_target_pairs={{8,0},{12,4},{16,8},{20,12},{24,16},{28,20},{32,24},{36,28},{40,32... | collective-permute-start | bytes 786440 | tf_op jit(solution)/shard_map/ppermute | solution.py:21
  48.4 1.1 copy-start.2
  102.5 96.0 %reduce-scatter.9.cloned.1.call-start = ((), (), s32[]{:S(2)}) async-start(), calls=%async_computation.5 | async-start | bytes 1310720
  146.9 13.5 %copy-start.4 = (bf16[512,512]{1,0:T(8,128)(2,1)S(1)}, bf16[512,512]{1,0:T(8,128)(2,1)}, u32[]{:S(2)}) copy-start(bf16[512,512]{1,0:T(8,128)(2,1)} %param.14) | copy-start | bytes 1572868
  163.0 1.4 copy-start.3
Sparse Core Ops, SparseCore 0:
  102.7 34.8 reduce-scatter.6
  164.5 33.9 reduce-scatter.8
